TPU v7x, 32 devices: a whole 2x2x4 slice. The times are simulated.
32 devices in a mesh: seq: 8 (over z, x), head: 4 (over y, core).
Axes of the slice: x: 2, y: 2, z: 4, core: 2. Of those that a mesh axis runs over, the one named last changes fastest.
Arguments:
- queries: bfloat16 [2048, 1024], P('seq', 'head'), may hold values from -40 to 40
- keys: bfloat16 [2048, 1024], P('seq', 'head'), may hold values from -12 to 12
- values: bfloat16 [2048, 1024], P('seq', 'head'), may hold values from -6 to 6
- residual: bfloat16 [2048, 1024], P('seq', 'head'), may hold values from -3 to 3
- reg_weight: bfloat16 [1024, 1024], P('head'), may hold values from -0.1875 to 0.1875
- targets: bfloat16 [32, 16, 1024], P('seq'), may hold values from -3 to 3
- block_track: int32 [16], replicated, may hold values from 0 to 31
- row_count: int32 [16], P('seq'), may hold values from 1 to 128, 1536 in all
- pool_slot: int32 [16, 128], P('seq'), may hold values from 0 to 15
Outputs:
- grad_reg: bfloat16 [1024, 1024], P('head')
- context_grad: bfloat16 [2048, 1024], P('seq', 'head')
All inputs are finite; a program needn't handle non-finite values. No bound on the sum of `row_count` on one device may be relied on, other than what follows from the above.
Results may differ from a plain program's by a relative error of at most 0.019.
Values may be sent and summed in bfloat16 or wider, within the bound.
A program may use at most 128 MiB of HBM per device.

v0:
```python
import jax
import jax.numpy as jnp
from jax import lax
from jax.sharding import PartitionSpec as P

HEAD_DIM = 64
BLK = 128
POOL = 16


def make_advance(query_heads, scale):

    def advance(state, block):
        run_max, run_total, run_sum = state
        key_rows, value_rows = block
        scores = (
            jnp.einsum("qhd,khd->hqk", query_heads, key_rows, preferred_element_type=jnp.float32)
            * scale
        )
        new_max = jnp.maximum(run_max, jnp.max(scores, axis=2))
        shrink = jnp.exp(run_max - new_max)
        exp_terms = jnp.exp(scores - new_max[:, :, None])
        run_total = run_total * shrink + jnp.sum(exp_terms, axis=2)
        weighted = jnp.einsum(
            "hqk,khd->hqd",
            exp_terms.astype(jnp.bfloat16),
            value_rows,
            preferred_element_type=jnp.float32,
        )
        run_sum = run_sum * shrink[:, :, None] + weighted
        return ((new_max, run_total, run_sum), None)

    return advance


def local(queries, keys, values, residual, reg_weight, targets, block_track, row_count, pool_slot):
    tok_rows, width = queries.shape
    head_count = width // HEAD_DIM
    query_heads = queries.reshape(tok_rows, head_count, HEAD_DIM)
    advance = make_advance(query_heads, HEAD_DIM ** (-0.5))
    initial = (
        jnp.full((head_count, tok_rows), -1e30, jnp.float32),
        jnp.zeros((head_count, tok_rows), jnp.float32),
        jnp.zeros((head_count, tok_rows, HEAD_DIM), jnp.float32),
    )
    state = initial
    key_piece = lax.all_gather(keys, "seq", axis=0, tiled=True)
    value_piece = lax.all_gather(values, "seq", axis=0, tiled=True)
    key_count = key_piece.shape[0]
    key_heads = key_piece.reshape(key_count, head_count, HEAD_DIM)
    value_heads = value_piece.reshape(key_count, head_count, HEAD_DIM)
    block_count = key_count // 512
    blocks = (
        key_heads.reshape(block_count, 512, head_count, HEAD_DIM),
        value_heads.reshape(block_count, 512, head_count, HEAD_DIM),
    )
    state, unused = lax.scan(advance, state, blocks)
    run_max, run_total, run_sum = state
    context = (
        (run_sum / run_total[:, :, None])
        .transpose(1, 0, 2)
        .reshape(tok_rows, width)
        .astype(jnp.bfloat16)
    )
    stream = (residual.astype(jnp.float32) + context.astype(jnp.float32)).astype(jnp.bfloat16)
    block_here = tok_rows // BLK
    owned = 2 * block_here
    seq_count = lax.axis_size("seq")
    tracks_all = owned * seq_count
    seq_index = lax.axis_index("seq")
    stream_blocks = stream.reshape(block_here, BLK, width)
    valid = jnp.arange(BLK, dtype=jnp.int32)[None, :] < row_count[:, None]
    match = pool_slot[:, None, :] == jnp.arange(POOL, dtype=jnp.int32)[None, :, None]
    selector = jnp.where(match & valid[:, None, :], 1.0, 0.0).astype(jnp.bfloat16)
    pooled = jnp.einsum("bpr,brc->bpc", selector, stream_blocks, preferred_element_type=jnp.float32)
    slot_rows = jnp.sum(selector.astype(jnp.float32), axis=2)
    own_track = lax.dynamic_slice_in_dim(block_track, seq_index * block_here, block_here)
    track_select = jnp.where(
        own_track[:, None] == jnp.arange(tracks_all, dtype=jnp.int32)[None, :], 1.0, 0.0
    ).astype(jnp.float32)
    dense_sums = jnp.einsum("bt,bpc->tpc", track_select, pooled, precision=lax.Precision.HIGHEST)
    dense_counts = jnp.einsum("bt,bp->tp", track_select, slot_rows, precision=lax.Precision.HIGHEST)
    sums, counts = (
        lax.psum_scatter(dense_sums, "seq", scatter_dimension=0, tiled=True),
        lax.psum_scatter(dense_counts, "seq", scatter_dimension=0, tiled=True),
    )
    divisor = jnp.maximum(counts, 1.0)
    mean = (sums / divisor[:, :, None]).astype(jnp.bfloat16).reshape(owned * POOL, width)
    partial_pred = jnp.dot(mean, reg_weight, preferred_element_type=jnp.float32)
    prediction = lax.psum(partial_pred.astype(jnp.bfloat16), "head").astype(jnp.float32)
    error = (prediction - targets.reshape(owned * POOL, -1).astype(jnp.float32)).astype(
        jnp.bfloat16
    )
    reg_part = lax.dot_general(
        mean, error, (((0,), (0,)), ((), ())), preferred_element_type=jnp.float32
    )
    mean_grad = lax.dot_general(
        error, reg_weight, (((1,), (1,)), ((), ())), preferred_element_type=jnp.float32
    )
    track_grad = (mean_grad.reshape(owned, POOL, width) / divisor[:, :, None]).astype(jnp.bfloat16)
    every_grad = lax.all_gather(track_grad, "seq", axis=0, tiled=True)
    grad_select = jnp.where(
        own_track[:, None] == jnp.arange(tracks_all, dtype=jnp.int32)[None, :], 1.0, 0.0
    ).astype(jnp.bfloat16)
    pooled_grad = jnp.einsum(
        "bt,tpc->bpc", grad_select, every_grad, preferred_element_type=jnp.float32
    ).astype(jnp.bfloat16)
    row_grad = jnp.einsum("bpr,bpc->brc", selector, pooled_grad, preferred_element_type=jnp.float32)
    context_grad = row_grad.reshape(tok_rows, width).astype(jnp.bfloat16)
    grad_reg = lax.psum(reg_part, "seq").astype(jnp.bfloat16)
    return (grad_reg, context_grad)


def solution(mesh):
    return jax.shard_map(
        local,
        mesh=mesh,
        in_specs=(
            P("seq", "head"),
            P("seq", "head"),
            P("seq", "head"),
            P("seq", "head"),
            P("head", None),
            P("seq", None, None),
            P(),
            P("seq"),
            P("seq", None),
        ),
        out_specs=(P("head", None), P("seq", "head")),
        check_vma=False,
    )
```

profile of v0, /device:TPU:0, one launch (start us, length us, event | category | flops | bytes accessed | tf_op | source)
XLA Modules:
  0.0 323.2 jit_solution(4602730668568704929)
XLA Ops:
  7.2 0.0 all-gather.3.cloned.1.call-start
  7.2 0.7 all-gather.3.cloned.1.call-update
  7.9 0.0 all-gather.5.cloned.1.call-start
  8.0 0.7 all-gather.5.cloned.1.call-update
  8.7 0.0 reduce-scatter.2.cloned.1.call-start
  8.7 1.0 copy.27
  9.8 0.7 dynamic_slice.10
  10.5 0.7 iota_compare_fusion.1
  11.2 41.8 %all-gather.3.cloned.1.call-done = bf16[2048,256]{1,0:T(8,128)(2,1)} async-done(((bf16[256,256]{1,0:T(8,128)(2,1)}), bf16[2048,256]{1,0:T(8,128)(2,1)}) %all-gather.3.cloned.1.call-update) | async-done | bytes 1048592 | tf_op jit(solution)/shard_map/all_gather | solution.py:47
  53.0 3.3 %reshape.56 = bf16[4,512,4,64]{3,2,1,0:T(4,128)(2,1)S(1)} reshape(bf16[2048,256]{1,0:T(8,128)(2,1)} %all-gather.3.cloned.1.call-done) | data formatting | bytes 2097152 | tf_op jit(solution)/shard_map/reshape;reshape | solution.py:54
  56.3 2.4 copy.29
  58.7 35.4 %all-gather.5.cloned.1.call-done = bf16[2048,256]{1,0:T(8,128)(2,1)} async-done(((bf16[256,256]{1,0:T(8,128)(2,1)}), bf16[2048,256]{1,0:T(8,128)(2,1)}) %all-gather.5.cloned.1.call-update) | async-done | bytes 1048592 | tf_op jit(solution)/shard_map/all_gather | solution.py:48
  94.1 3.3 %reshape.57 = bf16[4,512,4,64]{3,2,1,0:T(4,128)(2,1)S(1)} reshape(bf16[2048,256]{1,0:T(8,128)(2,1)} %all-gather.5.cloned.1.call-done) | data formatting | bytes 2097152 | tf_op jit(solution)/shard_map/reshape;reshape | solution.py:55
  97.4 2.3 copy.30
  99.8 13.5 %while.15 = (s32[]{:T(128)}, f32[4,256]{1,0:T(4,128)S(1)}, f32[4,256]{1,0:T(4,128)S(1)}, f32[4,256,64]{1,2,0:T(8,128)S(1)}, bf16[4,512,4,64]{1,3,2,0:T(8,128)(2,...) while((s32[]{:T(128)}, f32[4,256]{1,0:T(4,128)S(1)}, ...), condition=%wide.region_3.4_spmd.clone, body=%wide.region_0.3_spmd.clone.sunk | while | flops 138613760 | bytes 7537769 | solution.py:57
  99.8 1.5 bitcast_reduce_fusion.2
  101.3 0.4 fusion.74
  101.6 1.5 convolution_add_fusion.2
  103.1 1.5 bitcast_reduce_fusion.2
  104.6 0.4 fusion.74
  105.0 1.5 convolution_add_fusion.2
  106.5 1.5 bitcast_reduce_fusion.2
  108.0 0.4 fusion.74
  108.4 1.5 convolution_add_fusion.2
  109.9 1.5 bitcast_reduce_fusion.2
  111.3 0.4 fusion.74
  111.7 1.5 convolution_add_fusion.2
  113.3 0.1 copy.31
  113.5 0.1 fusion.22
  113.6 0.7 fusion.18
  114.3 1.1 copy.33
  115.5 0.0 all-reduce.4.cloned.1.call-start
  115.5 0.6 dynamic-slice
  116.8 0.1 convert_reduce_fusion
  116.8 0.3 fusion.33
  117.1 35.1 %all-reduce = f32[32,16]{1,0:T(8,128)S(1)} all-reduce(f32[32,16]{1,0:T(8,128)S(1)} %fusion.33), channel_id=3, replica_groups=mesh['seq'=8,'head'=4] {'seq'}, use_global_device_ids=true, to_apply=%region_6.7.clone | all-reduce | flops 512 | bytes 4096
  152.2 24.6 %reduce-scatter.2.cloned.1.call-done = f32[4,16,256]{2,1,0:T(8,128)} async-done(((f32[32,16,256]{2,1,0:T(8,128)}), f32[4,16,256]{2,1,0:T(8,128)}) %reduce-scatter.2.cloned.1.call-update) | async-done | bytes 65552 | tf_op jit(solution)/shard_map/reduce_scatter | solution.py:84
  176.8 0.9 divide_convert_fusion.2
  177.8 0.9 convolution_convert_fusion
  178.7 31.5 %all-reduce.4.cloned.1.call-done = bf16[64,1024]{1,0:T(8,128)(2,1)} async-done(((bf16[64,1024]{1,0:T(8,128)(2,1)}), bf16[64,1024]{1,0:T(8,128)(2,1)}) %all-reduce.4.cloned.1.call-update) | async-done | bytes 131088 | tf_op jit(solution)/shard_map/psum | solution.py:90
  210.1 0.9 fusion.15
  211.1 0.3 fusion.55
  211.4 0.3 fusion.56
  211.7 73.0 %all-reduce.5 = bf16[256,1024]{1,0:T(8,128)(2,1)} all-reduce(f32[256,1024]{1,0:T(8,128)S(1)} %fusion.55), channel_id=1, replica_groups=mesh['seq'=8,'head'=4] {'seq'}, use_global_device_ids=true, to_apply=%region_8.9 | all-reduce | flops 262144 | bytes 1572864 | tf_op jit(solution)/shard_map/psum | solution.py:110
  284.7 0.1 divide_convert_fusion.1
  284.8 30.7 %all_gather.11 = bf16[32,16,256]{2,1,0:T(8,128)(2,1)S(1)} all-gather(bf16[4,16,256]{2,1,0:T(8,128)(2,1)S(1)} %divide_convert_fusion.1), channel_id=1, replica_groups=mesh['seq'=8,'head'=4] {'seq'}, dimensions={0}, use_global_device_ids=true | all-gather | bytes 294912 | tf_op jit(solution)/shard_map/all_gather | solution.py:101
  315.6 0.2 convolution_convert_fusion.2
  315.8 0.9 convolution_convert_fusion.1
  (30 shorter events, 0.2 us)
Async XLA Ops:
  7.2 170.6 %copy-start = (bf16[256,1024]{1,0:T(8,128)(2,1)S(1)}, bf16[256,1024]{1,0:T(8,128)(2,1)}, u32[]{:S(2)}) copy-start(bf16[256,1024]{1,0:T(8,128)(2,1)} %param.15) | copy-start | bytes 1572868
  7.2 45.8 %all-gather.3.cloned.1.call-start = ((), (), s32[]{:S(2)}) async-start(), calls=%async_computation.1 | async-start | bytes 1179648 | tf_op jit(solution)/shard_map/all_gather | solution.py:47
  7.9 86.2 %all-gather.5.cloned.1.call-start = ((), (), s32[]{:S(2)}) async-start(), calls=%async_computation.2 | async-start | bytes 1179648 | tf_op jit(solution)/shard_map/all_gather | solution.py:48
  8.7 168.2 %reduce-scatter.2.cloned.1.call-start = ((), (), s32[]{:S(2)}) async-start(), calls=%async_computation.3 | async-start | bytes 589824 | tf_op jit(solution)/shard_map/reduce_scatter | solution.py:84
  99.8 13.7 %copy-start.2 = (bf16[256,256]{1,0:T(8,128)(2,1)S(1)}, bf16[256,256]{1,0:T(8,128)(2,1)}, u32[]{:S(2)}) copy-start(bf16[256,256]{1,0:T(8,128)(2,1)} %param.14) | copy-start | bytes 393220
  99.8 13.7 %copy-start.3 = (s32[2,128]{1,0:T(2,128)S(1)}, s32[2,128]{1,0:T(2,128)}, u32[]{:S(2)}) copy-start(s32[2,128]{1,0:T(2,128)} %param.19) | copy-start | bytes 3076
  113.2 2.3 copy-start.4
  113.3 96.9 %copy-start.1 = (bf16[4,16,1024]{2,1,0:T(8,128)(2,1)S(1)}, bf16[4,16,1024]{2,1,0:T(8,128)(2,1)}, u32[]{:S(2)}) copy-start(bf16[4,16,1024]{2,1,0:T(8,128)(2,1)} %param.16) | copy-start | bytes 393220
  115.5 94.7 %all-reduce.4.cloned.1.call-start = ((), (), s32[]{:S(2)}) async-start(), calls=%async_computation.4 | async-start | bytes 262144 | tf_op jit(solution)/shard_map/psum | solution.py:90
Sparse Core Ops, SparseCore 0:
  10.1 42.8 all-gather.2
  55.1 38.9 all-gather.4
  115.6 61.2 reduce-scatter.1
  179.7 30.3 all-reduce.3
where the time goes:
time: 324 us; the launch traced here: 323 us
  blocking collectives  139 us (43%)
  waiting for transfers between devices  135 us (42%)
  matrix products  15.4 us (5%)
  local copies, waits for them, and re-layouts  14.9 us (5%)
  between operations  14.6 us (5%)
  other arithmetic  4.37 us (1%)
    psum x1, blocking collectives, local(): grad_reg = lax.psum(reg_part, 'seq').astype(jnp.bfloat16)  73 us
    all_gather x1, waiting for transfers between devices, local(): key_piece = lax.all_gather(keys, 'seq', axis=0, tiled=True)  41.8 us
    all_gather x1, waiting for transfers between devices, local(): value_piece = lax.all_gather(values, 'seq', axis=0, tiled=True)  35.4 us
    unnamed x1, blocking collectives  35.1 us
    psum x1, waiting for transfers between devices, local(): lax.psum(partial_pred.astype(jnp.bfloat16), 'head').astype(jnp.float32)  31.5 us
    all_gather x1, blocking collectives, local(): every_grad = lax.all_gather(track_grad, 'seq', axis=0, tiled=True)  30.7 us
    reduce_scatter x1, waiting for transfers between devices, local(): lax.psum_scatter(dense_sums, 'seq', scatter_dimension=0, tiled=True)  24.6 us
  transfers between devices with their start and end apart: 4, of which 4 were waited for; matrix products, arithmetic and copies ran while one was open for 3% of the time, Pallas kernels for 0%

commit v1 on v0

v1 whole, which is shorter than its diff:
```python
import functools

import jax
import jax.numpy as jnp
from jax import lax
from jax.experimental import pallas as pl
from jax.experimental.pallas import tpu as pltpu
from jax.sharding import PartitionSpec as P

HEAD_DIM = 64
BLK = 128
POOL = 16
INFO = 16
BF = jnp.bfloat16
F32 = jnp.float32
MESH = pl.DeviceIdType.MESH
NT = (((1,), (1,)), ((), ()))
TN = (((0,), (0,)), ((), ()))


def drain(ref, sem):
    pltpu.make_async_copy(ref, ref, sem).wait()


def remote(src, dst, send, recv, seq, head):
    return pltpu.make_async_remote_copy(
        src_ref=src, dst_ref=dst, send_sem=send, recv_sem=recv,
        device_id={"seq": seq, "head": head}, device_id_type=MESH,
    )


def kernel(
    n, q_ref, k_ref, v_ref, r_ref, w_ref, tgt_ref, bt_ref, rc_ref, ps_ref,
    greg_ref, cgrad_ref,
    kvs, qrs, kvb, qrb, qx, vx, run_max, acc, wbuf, stream, sb, rb, ms, mb, es, eb, gacc,
    kv_send, kv_recv, qr_send, qr_recv, fw_send, w_send, w_recv,
    b_send, b_recv, m_send, m_recv, e_send, e_recv, ef_send, ef_recv,
):
    g = n // 8
    devices = 4 * n
    seq, head = lax.axis_index("seq"), lax.axis_index("head")
    core, yy = head % 2, head // 2
    partner, across = 2 * yy + 1 - core, (head + 2) % 4
    lin = seq * 4 + head
    tok = q_ref.shape[0]

    barrier = pltpu.get_barrier_semaphore()

    @pl.loop(1, devices)
    def _(i):
        other = (lin + i) % devices
        pl.semaphore_signal(
            barrier, inc=1, device_id={"seq": other // 4, "head": other % 4}, device_id_type=MESH
        )

    lane_row = lax.broadcasted_iota(jnp.int32, (1, BLK), 1)
    slots = [
        jnp.where(lane_row < rc_ref[b], ps_ref[b:b + 1, :], -1).astype(F32) for b in range(2)
    ]
    own_tracks = [bt_ref[2 * seq + b] for b in range(2)]
    row = lax.broadcasted_iota(jnp.int32, (INFO, BLK), 0)
    tracks = jnp.where(row == 2, own_tracks[0], own_tracks[1]).astype(F32)
    info = jnp.where(row == 0, slots[0], jnp.where(row == 1, slots[1], tracks)).astype(BF)
    for j in range(4):
        cols = slice(j * HEAD_DIM, (j + 1) * HEAD_DIM)
        qrs[j] = jnp.concatenate([q_ref[:, cols] * BF(HEAD_DIM ** -0.5), r_ref[:, cols]], axis=1)
        kvs[j, 0:tok, :] = jnp.concatenate([k_ref[:, cols], v_ref[:, cols]], axis=1)
        kvs[j, tok:tok + INFO, :] = info

    pl.semaphore_wait(barrier, devices - 1)

    half, chunk = (seq // 4) % 2, seq // 8
    to_head = 2 * yy + half

    def first_sends(act):
        for j in range(4):
            lead = (4 * core + j) * g
            here = jnp.logical_and(lead + chunk == seq, to_head == head)
            act(
                here,
                remote(qrs.at[j], qrb.at[seq % 4], qr_send.at[j], qr_recv, lead + chunk, to_head),
                pltpu.make_async_copy(qrs.at[j], qrb.at[seq % 4], qr_recv),
            )
            for c in range(g):
                here = jnp.logical_and(lead + c == seq, to_head == head)
                act(
                    here,
                    remote(kvs.at[j], kvb.at[seq], kv_send.at[j * g + c], kv_recv.at[seq],
                           lead + c, to_head),
                    pltpu.make_async_copy(kvs.at[j], kvb.at[seq], kv_recv.at[seq]),
                )

    def begin(here, far, near):
        @pl.when(here)
        def _():
            near.start()

        @pl.when(jnp.logical_not(here))
        def _():
            far.start()

    def finish(here, far, near):
        @pl.when(jnp.logical_not(here))
        def _():
            far.wait_send()

    first_sends(begin)
    w_across = remote(w_ref, wbuf.at[head], w_send.at[0], w_recv.at[head], seq, across)
    w_pair = remote(w_ref, wbuf.at[head], w_send.at[1], w_recv.at[head], seq, partner)
    w_own = pltpu.make_async_copy(w_ref, wbuf.at[head], w_recv.at[head])
    w_across.start()
    w_pair.start()
    w_own.start()

    run_max[...] = jnp.full_like(run_max, -1e30)
    acc[...] = jnp.zeros_like(acc)
    queries = qx.shape[0]
    low = lax.broadcasted_iota(jnp.int32, (1, 2 * HEAD_DIM), 1) < HEAD_DIM

    drain(qrb, qr_recv)
    flat = qrb[...].reshape(queries, 2 * HEAD_DIM)
    qx[...] = jnp.where(low, flat, jnp.zeros_like(flat))

    def attend(first):
        pair = kvb[pl.ds(first, 2), 0:tok, :].reshape(2 * tok, 2 * HEAD_DIM)
        vx[...] = jnp.where(low, jnp.ones_like(pair), pair)
        for t in range(queries // 256):
            rows = slice(t * 256, (t + 1) * 256)
            scores = lax.dot_general(qx[rows, :], pair, NT, preferred_element_type=F32)
            old = run_max[rows, :]
            new = jnp.maximum(old, jnp.max(scores, axis=1, keepdims=True))
            weights = jnp.exp(scores - new[:, 0:1]).astype(BF)
            acc[rows, :] = acc[rows, :] * jnp.exp(old - new) + jnp.dot(
                weights, vx[...], preferred_element_type=F32
            )
            run_max[rows, :] = new

    @pl.loop(0, n // 4)
    def _(i):
        first = (i // 2) * 8 + 4 * core + 2 * (i % 2)
        for one in range(2):
            s = first + one
            drain(kvb.at[s], kv_recv.at[s])
            remote(kvb.at[s], kvb.at[s], fw_send, kv_recv.at[s], seq, partner).start()
        attend(first)

    @pl.loop(0, n // 4)
    def _(i):
        first = (i // 2) * 8 + 4 * (1 - core) + 2 * (i % 2)
        for one in range(2):
            drain(kvb.at[first + one], kv_recv.at[first + one])
        attend(first)

    drain(wbuf.at[across], w_recv.at[across])
    w_on = remote(wbuf.at[across], wbuf.at[across], w_send.at[2], w_recv.at[across], seq, partner)
    w_on.start()

    def codes_of(s):
        lines = kvb[s, tok:tok + INFO, :].astype(F32)
        return [
            jnp.where(lines[b:b + 1] < 0, -1.0, POOL * lines[2 + b:3 + b] + lines[b:b + 1])
            for b in range(2)
        ]

    total = acc[...]
    context = (total / pltpu.roll(total, HEAD_DIM, 1)).astype(BF).astype(F32)
    summed = (qrb[...].reshape(queries, 2 * HEAD_DIM).astype(F32) + context).astype(BF)
    stream[...] = jnp.where(low, jnp.zeros_like(summed), summed)

    here_first = (seq % g) * 8 + 4 * core
    here_codes = [code for i in range(4) for code in codes_of(here_first + i)]
    big_rows = lax.broadcasted_iota(jnp.int32, (512, BLK), 0).astype(F32)

    @pl.loop(0, devices // 32)
    def _(i):
        base = (i * 512).astype(F32)
        pick = jnp.concatenate(
            [jnp.where(big_rows == code - base, 1.0, 0.0).astype(BF) for code in here_codes],
            axis=1,
        )
        part = jnp.dot(pick, stream[...], preferred_element_type=F32)
        part = part.reshape(32, POOL, 2 * HEAD_DIM)
        upper, lower = part[:, 0:8, :], part[:, 8:16, :]
        turned = pltpu.roll(lower.reshape(256, 2 * HEAD_DIM), HEAD_DIM, 1)
        sb[pl.ds(i * 32, 32)] = jnp.where(low, turned, upper.reshape(256, 2 * HEAD_DIM)).reshape(
            32, 8, 2 * HEAD_DIM
        )

    @pl.loop(1, devices)
    def _(i):
        t = (lin + i) % devices
        remote(sb.at[t], rb.at[lin], b_send, b_recv, t // 4, t % 4).start()

    pltpu.make_async_copy(sb.at[lin], rb.at[lin], b_recv).start()

    slot_row = lax.broadcasted_iota(jnp.int32, (POOL, BLK), 0)
    wanted = [(t * POOL + slot_row).astype(F32) for t in (lin, own_tracks[0], own_tracks[1])]

    def add_counts(s, sums):
        codes = codes_of(s)
        return tuple(
            total + jnp.where(want == codes[0], 1.0, 0.0) + jnp.where(want == codes[1], 1.0, 0.0)
            for total, want in zip(sums, wanted)
        )

    zero = jnp.zeros((POOL, BLK), F32)
    counts = lax.fori_loop(0, n, add_counts, (zero, zero, zero))
    divisors = [jnp.maximum(jnp.sum(c, axis=1, keepdims=True), 1.0) for c in counts]

    drain(rb, b_recv)
    tiles = []
    for pair in range(8):
        sides = []
        for hd in (2 * pair, 2 * pair + 1):
            y, h = hd // 8, hd % 8
            side = None
            for c in range(2):
                for part in range(g):
                    piece = rb[(h * g + part) * 4 + 2 * y + c]
                    side = piece if side is None else side + piece
            sides.append(side)
        a, b = sides
        upper = jnp.where(low, pltpu.roll(a, HEAD_DIM, 1), b)
        lower = jnp.where(low, a, pltpu.roll(b, HEAD_DIM, 1))
        tiles.append((jnp.concatenate([upper, lower], axis=0) / divisors[0]).astype(BF))
    for k in range(4):
        ms[k] = jnp.concatenate(tiles[2 * k:2 * k + 2], axis=1)

    place = core * 2 * n + seq * 2 + yy

    @pl.loop(1, devices)
    def _(i):
        t = (lin + i) % devices
        remote(ms.at[t % 4], mb.at[place], m_send, m_recv, t // 4, t % 4).start()

    pltpu.make_async_copy(ms.at[head], mb.at[place], m_recv).start()

    for k in range(2):
        drain(wbuf.at[2 * yy + k], w_recv.at[2 * yy + k])
    drain(wbuf.at[2 * (1 - yy) + 1 - core], w_recv.at[2 * (1 - yy) + 1 - core])
    prediction = jnp.dot(ms[0], wbuf[0], preferred_element_type=F32)
    for k in range(1, 4):
        prediction += jnp.dot(ms[k], wbuf[k], preferred_element_type=F32)
    es[...] = (prediction - tgt_ref[head].astype(F32)).astype(BF)

    @pl.loop(1, 2 * n)
    def _(i):
        spot = (seq * 2 + yy + i) % (2 * n)
        remote(es, eb.at[place], e_send, e_recv, spot // 2, 2 * (spot % 2) + core).start()

    pltpu.make_async_copy(es, eb.at[place], e_recv).start()

    drain(mb, m_recv)
    mine, theirs = pl.ds(core * 2 * n, 2 * n), pl.ds((1 - core) * 2 * n, 2 * n)
    drain(eb.at[mine], e_recv)
    e_on = remote(eb.at[mine], eb.at[mine], ef_send, ef_recv, seq, partner)
    e_on.start()

    own_code = jnp.concatenate(
        [(t * POOL + lax.broadcasted_iota(jnp.int32, (POOL, 1), 0)) for t in own_tracks], axis=0
    )
    picked = jnp.zeros((2 * POOL, es.shape[1]), F32)
    for turn in range(2):
        side = core if turn == 0 else 1 - core
        if turn == 1:
            drain(eb.at[theirs], ef_recv)

        def gather(i, picked, side=side, fresh=turn == 0):
            begin_at = side * 2 * n + i * 16
            means = mb[pl.ds(begin_at, 16)].reshape(256, -1)
            errors = eb[pl.ds(begin_at, 16)].reshape(256, -1)
            term = lax.dot_general(means, errors, TN, preferred_element_type=F32)
            if fresh:
                gacc[...] = term + jnp.where(i > 0, gacc[...], 0.0)
            else:
                gacc[...] += term
            spot = lax.broadcasted_iota(jnp.int32, (2 * POOL, 256), 1)
            where = i * 16 + spot // POOL
            code = (2 * where + side) * POOL + spot % POOL
            pick = jnp.where(code == own_code, 1.0, 0.0).astype(BF)
            return picked + jnp.dot(pick, errors, preferred_element_type=F32)

        picked = lax.fori_loop(0, n // 8, gather, picked)

    greg_ref[...] = gacc[...].astype(BF)
    mean_grad = lax.dot_general(picked.astype(BF), w_ref[...], NT, preferred_element_type=F32)
    track_grad = (mean_grad / jnp.concatenate(divisors[1:], axis=0)).astype(BF)
    for b in range(2):
        select = jnp.where(slot_row.astype(F32) == slots[b], 1.0, 0.0).astype(BF)
        cgrad_ref[b * BLK:(b + 1) * BLK, :] = lax.dot_general(
            select, track_grad[b * POOL:(b + 1) * POOL], TN, preferred_element_type=F32
        ).astype(BF)

    first_sends(finish)
    drain(kvb.at[pl.ds(0, n // 2)], fw_send)
    w_across.wait_send()
    w_pair.wait_send()
    w_on.wait_send()
    drain(sb.at[pl.ds(0, devices - 1)], b_send)
    drain(mb.at[pl.ds(0, devices - 1)], m_send)
    drain(eb.at[pl.ds(0, 2 * n - 1)], e_send)
    e_on.wait_send()


def solution(mesh):
    n = mesh.shape["seq"]
    devices = 4 * n

    def local(queries, keys, values, residual, weight, targets, block_track, row_count, slot):
        tok, width = queries.shape
        target_width = weight.shape[1]
        dma = pltpu.SemaphoreType.DMA
        vmem, smem = pl.BlockSpec(memory_space=pltpu.VMEM), pl.BlockSpec(memory_space=pltpu.SMEM)
        two = 2 * HEAD_DIM
        return pl.pallas_call(
            functools.partial(kernel, n),
            out_shape=(
                jax.ShapeDtypeStruct((width, target_width), BF),
                jax.ShapeDtypeStruct((tok, width), BF),
            ),
            in_specs=[vmem] * 6 + [smem, smem, vmem],
            out_specs=(vmem, vmem),
            scratch_shapes=[
                pltpu.VMEM((4, tok + INFO, two), BF),
                pltpu.VMEM((4, tok, two), BF),
                pltpu.VMEM((n, tok + INFO, two), BF),
                pltpu.VMEM((4, tok, two), BF),
                pltpu.VMEM((4 * tok, two), BF),
                pltpu.VMEM((2 * tok, two), BF),
                pltpu.VMEM((4 * tok, two), F32),
                pltpu.VMEM((4 * tok, two), F32),
                pltpu.VMEM((4, width, target_width), BF),
                pltpu.VMEM((4 * tok, two), BF),
                pltpu.VMEM((devices, 8, two), F32),
                pltpu.VMEM((devices, 8, two), F32),
                pltpu.VMEM((4, POOL, width), BF),
                pltpu.VMEM((devices, POOL, width), BF),
                pltpu.VMEM((POOL, target_width), BF),
                pltpu.VMEM((devices, POOL, target_width), BF),
                pltpu.VMEM((width, target_width), F32),
                dma((4 * (n // 8),)),
                dma((n,)),
                dma((4,)),
                dma,
                dma,
                dma((3,)),
                dma((4,)),
                dma, dma, dma, dma, dma, dma, dma, dma,
            ],
            compiler_params=pltpu.CompilerParams(
                collective_id=0, has_side_effects=True, vmem_limit_bytes=56 * 1024 * 1024
            ),
            cost_estimate=pl.CostEstimate(
                flops=4 * 4 * tok * n * tok * HEAD_DIM, bytes_accessed=8 * 1024 * 1024,
                transcendentals=4 * tok * n * tok,
            ),
        )(queries, keys, values, residual, weight, targets, block_track, row_count, slot)

    return jax.shard_map(
        local,
        mesh=mesh,
        in_specs=(
            P("seq", "head"),
            P("seq", "head"),
            P("seq", "head"),
            P("seq", "head"),
            P("head", None),
            P("seq", None, None),
            P(),
            P("seq"),
            P("seq", None),
        ),
        out_specs=(P("head", None), P("seq", "head")),
        check_vma=False,
    )
```

time: 324 us -> 59.3 us (0.18)
  the two profiles are of different devices: /device:TPU:0 before, /device:TPU:11 now
where the time goes in v1:
time: 59.3 us; the launch traced here: 59.2 us
  Pallas kernels  55.9 us (94%)
  local copies, waits for them, and re-layouts  2.56 us (4%)
  between operations  0.65 us (1%)
    pallas_call x1, Pallas kernels, local(): pl.pallas_call(functools.partial(kernel, n), out_shape=(jax.ShapeDtypeStr...  55.9 us
    unnamed x4, local copies, waits for them, and re-layouts  2.56 us

profile of v1, /device:TPU:11, one launch (start us, length us, event | category | flops | bytes accessed | tf_op | source)
XLA Modules:
  0.0 59.2 jit_solution(8891862242440183147)
XLA Ops:
  0.6 55.9 %shard_map.104 = (bf16[256,1024]{1,0:T(8,128)(2,1)}, bf16[256,256]{1,0:T(8,128)(2,1)}) custom-call(bf16[256,256]{1,0:T(8,128)(2,1)} %q_ref.1, bf16[256,256]{1,0:T(8,128)(2,1)} %k_ref.1, bf16[256,256]{1,0:T(8,128)(2,1)} %v_ref.1, bf16[256,256]{1,0:T(8,128)(2,1)} %r_ref.1, bf16[256,1024]{1,0:T(8,128)(2,1)} %w_ref.1, bf16[4,16,1024]{2,1,0:T(8,128)(2,1)} %tgt_ref.1, ...), custom_call_target="tpu_custom_call" | custom-call | flops 536870912 | bytes 8388608 | tf_op jit(solution)/shard_map/pallas_call | solution.py:315
  56.6 0.0 copy-start
  56.6 1.9 %copy.13 = bf16[256,1024]{1,0:T(8,128)(2,1)} copy(bf16[256,1024]{1,0:T(8,128)(2,1)} %get-tuple-element.4) | data formatting | bytes 1048576
  58.5 0.0 copy-done
  58.5 0.7 %copy.14 = bf16[256,256]{1,0:T(8,128)(2,1)} copy(bf16[256,256]{1,0:T(8,128)(2,1)S(1)} %copy-done) | data formatting | bytes 262144
Async XLA Ops:
  56.6 1.9 %copy-start = (bf16[256,256]{1,0:T(8,128)(2,1)S(1)}, bf16[256,256]{1,0:T(8,128)(2,1)}, u32[]{:S(2)}) copy-start(bf16[256,256]{1,0:T(8,128)(2,1)} %get-tuple-element.5) | copy-start | bytes 393220

commit v2 on v1

--- a/solution.py
+++ b/solution.py
@@ -32,9 +32,10 @@
 def kernel(
     n, q_ref, k_ref, v_ref, r_ref, w_ref, tgt_ref, bt_ref, rc_ref, ps_ref,
     greg_ref, cgrad_ref,
-    kvs, qrs, kvb, qrb, qx, vx, run_max, acc, wbuf, stream, sb, rb, ms, mb, es, eb, gacc,
+    kvs, qrs, kvb, qrb, qx, vx, run_max, acc, wbuf, stream, sb, rb, m1, mb, eb, gacc,
     kv_send, kv_recv, qr_send, qr_recv, fw_send, w_send, w_recv,
-    b_send, b_recv, m_send, m_recv, e_send, e_recv, ef_send, ef_recv,
+    b_send, b_recv, m_send, m_recv, m2_send, m2_recv, e_send, e_recv, e2_send, e2_recv,
+    ef_send, ef_recv,
 ):
     g = n // 8
     devices = 4 * n
@@ -75,16 +76,16 @@
     def first_sends(act):
         for j in range(4):
             lead = (4 * core + j) * g
-            here = jnp.logical_and(lead + chunk == seq, to_head == head)
             act(
-                here,
+                jnp.logical_and(lead + chunk == seq, to_head == head),
                 remote(qrs.at[j], qrb.at[seq % 4], qr_send.at[j], qr_recv, lead + chunk, to_head),
                 pltpu.make_async_copy(qrs.at[j], qrb.at[seq % 4], qr_recv),
             )
+        for j in range(4):
+            lead = (4 * core + j) * g
             for c in range(g):
-                here = jnp.logical_and(lead + c == seq, to_head == head)
                 act(
-                    here,
+                    jnp.logical_and(lead + c == seq, to_head == head),
                     remote(kvs.at[j], kvb.at[seq], kv_send.at[j * g + c], kv_recv.at[seq],
                            lead + c, to_head),
                     pltpu.make_async_copy(kvs.at[j], kvb.at[seq], kv_recv.at[seq]),
@@ -223,52 +224,89 @@
         upper = jnp.where(low, pltpu.roll(a, HEAD_DIM, 1), b)
         lower = jnp.where(low, a, pltpu.roll(b, HEAD_DIM, 1))
         tiles.append((jnp.concatenate([upper, lower], axis=0) / divisors[0]).astype(BF))
+    line = n // 2
+    outer, inner = seq // 2, seq % 2
+    sign = 1 - 2 * (outer // (line // 2))
+    block = inner * 2 + yy
+    mean = [jnp.concatenate(tiles[2 * k:2 * k + 2], axis=1) for k in range(4)]
     for k in range(4):
-        ms[k] = jnp.concatenate(tiles[2 * k:2 * k + 2], axis=1)
-
-    place = core * 2 * n + seq * 2 + yy
-
-    @pl.loop(1, devices)
-    def _(i):
-        t = (lin + i) % devices
-        remote(ms.at[t % 4], mb.at[place], m_send, m_recv, t // 4, t % 4).start()
-
-    pltpu.make_async_copy(ms.at[head], mb.at[place], m_recv).start()
+        m1[k, outer] = mean[k]
+
+    def along(i):
+        return (outer + sign * i + line) % line
+
+    def plane(d):
+        return (inner + d % 2) % 2, (yy + d // 2) % 2
+
+    @pl.loop(1, line)
+    def _(i):
+        spot = m1.at[:, outer]
+        remote(spot, spot, m_send, m_recv, along(i) * 2 + inner, head).start()
 
     for k in range(2):
         drain(wbuf.at[2 * yy + k], w_recv.at[2 * yy + k])
     drain(wbuf.at[2 * (1 - yy) + 1 - core], w_recv.at[2 * (1 - yy) + 1 - core])
-    prediction = jnp.dot(ms[0], wbuf[0], preferred_element_type=F32)
+    prediction = jnp.dot(mean[0], wbuf[0], preferred_element_type=F32)
     for k in range(1, 4):
-        prediction += jnp.dot(ms[k], wbuf[k], preferred_element_type=F32)
-    es[...] = (prediction - tgt_ref[head].astype(F32)).astype(BF)
-
-    @pl.loop(1, 2 * n)
-    def _(i):
-        spot = (seq * 2 + yy + i) % (2 * n)
-        remote(es, eb.at[place], e_send, e_recv, spot // 2, 2 * (spot % 2) + core).start()
-
-    pltpu.make_async_copy(es, eb.at[place], e_recv).start()
-
-    drain(mb, m_recv)
-    mine, theirs = pl.ds(core * 2 * n, 2 * n), pl.ds((1 - core) * 2 * n, 2 * n)
-    drain(eb.at[mine], e_recv)
-    e_on = remote(eb.at[mine], eb.at[mine], ef_send, ef_recv, seq, partner)
-    e_on.start()
+        prediction += jnp.dot(mean[k], wbuf[k], preferred_element_type=F32)
+    error_at = eb.at[core, block * line + outer]
+    error_at[...] = (prediction - tgt_ref[head].astype(F32)).astype(BF)
+
+    @pl.loop(1, line)
+    def _(i):
+        remote(
+            error_at, error_at, e_send, e_recv.at[outer], along(i) * 2 + inner, head
+        ).start()
+
+    drain(m1.at[:, 0:line - 1], m_recv)
+    mean_to = mb.at[core, pl.ds(block * line, line)]
+    for d in range(4):
+        to_inner, to_yy = plane(d)
+        for c in range(2):
+            to = 2 * to_yy + (core if c == 0 else 1 - core)
+            if d == 0 and c == 0:
+                pltpu.make_async_copy(m1.at[to], mean_to, m2_recv).start()
+            else:
+                remote(m1.at[to], mean_to, m2_send, m2_recv, outer * 2 + to_inner, to).start()
+
+    @pl.loop(0, line)
+    def _(i):
+        spot = block * line + along(i)
+
+        @pl.when(i > 0)
+        def _():
+            drain(eb.at[core, spot], e_recv.at[along(i)])
+
+        for d in range(1, 4):
+            to_inner, to_yy = plane(d)
+            remote(
+                eb.at[core, spot], eb.at[core, spot], e2_send, e2_recv.at[block],
+                outer * 2 + to_inner, 2 * to_yy + core,
+            ).start()
+
+    for d in range(4):
+        from_inner, from_yy = plane(d)
+        other = from_inner * 2 + from_yy
+        part = eb.at[core, pl.ds(other * line, line)]
+        if d > 0:
+            drain(part, e2_recv.at[other])
+        remote(part, part, ef_send, ef_recv.at[other], seq, partner).start()
+
+    drain(mb, m2_recv)
 
     own_code = jnp.concatenate(
         [(t * POOL + lax.broadcasted_iota(jnp.int32, (POOL, 1), 0)) for t in own_tracks], axis=0
     )
-    picked = jnp.zeros((2 * POOL, es.shape[1]), F32)
+    picked = jnp.zeros((2 * POOL, w_ref.shape[1]), F32)
     for turn in range(2):
         side = core if turn == 0 else 1 - core
         if turn == 1:
-            drain(eb.at[theirs], ef_recv)
+            for o in range(4):
+                drain(eb.at[side, pl.ds(o * line, line)], ef_recv.at[o])
 
         def gather(i, picked, side=side, fresh=turn == 0):
-            begin_at = side * 2 * n + i * 16
-            means = mb[pl.ds(begin_at, 16)].reshape(256, -1)
-            errors = eb[pl.ds(begin_at, 16)].reshape(256, -1)
+            means = mb[side, pl.ds(i * 16, 16)].reshape(256, -1)
+            errors = eb[side, pl.ds(i * 16, 16)].reshape(256, -1)
             term = lax.dot_general(means, errors, TN, preferred_element_type=F32)
             if fresh:
                 gacc[...] = term + jnp.where(i > 0, gacc[...], 0.0)
@@ -276,7 +314,8 @@
                 gacc[...] += term
             spot = lax.broadcasted_iota(jnp.int32, (2 * POOL, 256), 1)
             where = i * 16 + spot // POOL
-            code = (2 * where + side) * POOL + spot % POOL
+            track = 4 * (2 * (where % line) + where // (2 * line)) + 2 * (where // line % 2) + side
+            code = track * POOL + spot % POOL
             pick = jnp.where(code == own_code, 1.0, 0.0).astype(BF)
             return picked + jnp.dot(pick, errors, preferred_element_type=F32)
 
@@ -297,9 +336,11 @@
     w_pair.wait_send()
     w_on.wait_send()
     drain(sb.at[pl.ds(0, devices - 1)], b_send)
-    drain(mb.at[pl.ds(0, devices - 1)], m_send)
-    drain(eb.at[pl.ds(0, 2 * n - 1)], e_send)
-    e_on.wait_send()
+    drain(m1.at[:, 0:line - 1], m_send)
+    drain(eb.at[0, 0:7 * line // 4], m2_send)
+    drain(eb.at[0, 0:line - 1], e_send)
+    drain(eb.at[0, 0:3 * line], e2_send)
+    drain(eb.at[0], ef_send)
 
 
 def solution(mesh):
@@ -333,10 +374,9 @@
                 pltpu.VMEM((4 * tok, two), BF),
                 pltpu.VMEM((devices, 8, two), F32),
                 pltpu.VMEM((devices, 8, two), F32),
-                pltpu.VMEM((4, POOL, width), BF),
-                pltpu.VMEM((devices, POOL, width), BF),
-                pltpu.VMEM((POOL, target_width), BF),
-                pltpu.VMEM((devices, POOL, target_width), BF),
+                pltpu.VMEM((4, n // 2, POOL, width), BF),
+                pltpu.VMEM((2, 2 * n, POOL, width), BF),
+                pltpu.VMEM((2, 2 * n, POOL, target_width), BF),
                 pltpu.VMEM((width, target_width), F32),
                 dma((4 * (n // 8),)),
                 dma((n,)),
@@ -345,7 +385,8 @@
                 dma,
                 dma((3,)),
                 dma((4,)),
-                dma, dma, dma, dma, dma, dma, dma, dma,
+                dma, dma, dma, dma, dma, dma,
+                dma, dma((n // 2,)), dma, dma((4,)), dma, dma((4,)),
             ],
             compiler_params=pltpu.CompilerParams(
                 collective_id=0, has_side_effects=True, vmem_limit_bytes=56 * 1024 * 1024

time: 59.3 us -> 56 us (0.944)
  the two profiles are of different devices: /device:TPU:11 before, /device:TPU:0 now
where the time goes in v2:
time: 56 us; the launch traced here: 55.2 us
  Pallas kernels  52 us (93%)
  local copies, waits for them, and re-layouts  2.56 us (5%)
  between operations  0.65 us (1%)
    pallas_call x1, Pallas kernels, local(): pl.pallas_call(functools.partial(kernel, n), out_shape=(jax.ShapeDtypeStr...  52 us
    unnamed x4, local copies, waits for them, and re-layouts  2.56 us

profile of v2, /device:TPU:0, one launch (start us, length us, event | category | flops | bytes accessed | tf_op | source)
XLA Modules:
  0.0 55.2 jit_solution(4193850487883280771)
XLA Ops:
  0.6 52.0 %shard_map.104 = (bf16[256,1024]{1,0:T(8,128)(2,1)}, bf16[256,256]{1,0:T(8,128)(2,1)}) custom-call(bf16[256,256]{1,0:T(8,128)(2,1)} %q_ref.1, bf16[256,256]{1,0:T(8,128)(2,1)} %k_ref.1, bf16[256,256]{1,0:T(8,128)(2,1)} %v_ref.1, bf16[256,256]{1,0:T(8,128)(2,1)} %r_ref.1, bf16[256,1024]{1,0:T(8,128)(2,1)} %w_ref.1, bf16[4,16,1024]{2,1,0:T(8,128)(2,1)} %tgt_ref.1, ...), custom_call_target="tpu_custom_call" | custom-call | flops 536870912 | bytes 8388608 | tf_op jit(solution)/shard_map/pallas_call | solution.py:356
  52.6 0.0 copy-start
  52.6 1.9 %copy.13 = bf16[256,1024]{1,0:T(8,128)(2,1)} copy(bf16[256,1024]{1,0:T(8,128)(2,1)} %get-tuple-element.4) | data formatting | bytes 1048576
  54.5 0.0 copy-done
  54.5 0.7 %copy.14 = bf16[256,256]{1,0:T(8,128)(2,1)} copy(bf16[256,256]{1,0:T(8,128)(2,1)S(1)} %copy-done) | data formatting | bytes 262144
Async XLA Ops:
  52.6 1.9 %copy-start = (bf16[256,256]{1,0:T(8,128)(2,1)S(1)}, bf16[256,256]{1,0:T(8,128)(2,1)}, u32[]{:S(2)}) copy-start(bf16[256,256]{1,0:T(8,128)(2,1)} %get-tuple-element.5) | copy-start | bytes 393220

commit v3 on v2

--- a/solution.py
+++ b/solution.py
@@ -31,9 +31,9 @@
 
 def kernel(
     n, q_ref, k_ref, v_ref, r_ref, w_ref, tgt_ref, bt_ref, rc_ref, ps_ref,
-    greg_ref, cgrad_ref,
-    kvs, qrs, kvb, qrb, qx, vx, run_max, acc, wbuf, stream, sb, rb, m1, mb, eb, gacc,
-    kv_send, kv_recv, qr_send, qr_recv, fw_send, w_send, w_recv,
+    greg_ref, tgrad_ref,
+    kvs, qs, rs, kvb, qb, rb_in, qx, rx, vxt, run_max, acc, wbuf, sb, rb, m1, mb, eb, gacc,
+    kv_send, kv_recv, q_send, q_recv, r_send, r_recv, fw_send, w_send, w_recv,
     b_send, b_recv, m_send, m_recv, m2_send, m2_recv, e_send, e_recv, e2_send, e2_recv,
     ef_send, ef_recv,
 ):
@@ -64,7 +64,8 @@
     info = jnp.where(row == 0, slots[0], jnp.where(row == 1, slots[1], tracks)).astype(BF)
     for j in range(4):
         cols = slice(j * HEAD_DIM, (j + 1) * HEAD_DIM)
-        qrs[j] = jnp.concatenate([q_ref[:, cols] * BF(HEAD_DIM ** -0.5), r_ref[:, cols]], axis=1)
+        qs[j] = jnp.concatenate([q_ref[0:BLK, cols], q_ref[BLK:, cols]], axis=1) * BF(HEAD_DIM ** -0.5)
+        rs[j] = jnp.concatenate([r_ref[0:BLK, cols], r_ref[BLK:, cols]], axis=1)
         kvs[j, 0:tok, :] = jnp.concatenate([k_ref[:, cols], v_ref[:, cols]], axis=1)
         kvs[j, tok:tok + INFO, :] = info
 
@@ -74,13 +75,16 @@
     to_head = 2 * yy + half
 
     def first_sends(act):
-        for j in range(4):
-            lead = (4 * core + j) * g
-            act(
-                jnp.logical_and(lead + chunk == seq, to_head == head),
-                remote(qrs.at[j], qrb.at[seq % 4], qr_send.at[j], qr_recv, lead + chunk, to_head),
-                pltpu.make_async_copy(qrs.at[j], qrb.at[seq % 4], qr_recv),
-            )
+        def whole(src, dst, send, recv):
+            for j in range(4):
+                lead = (4 * core + j) * g + chunk
+                act(
+                    jnp.logical_and(lead == seq, to_head == head),
+                    remote(src.at[j], dst.at[seq % 4], send.at[j], recv, lead, to_head),
+                    pltpu.make_async_copy(src.at[j], dst.at[seq % 4], recv),
+                )
+
+        whole(qs, qb, q_send, q_recv)
         for j in range(4):
             lead = (4 * core + j) * g
             for c in range(g):
@@ -90,6 +94,7 @@
                            lead + c, to_head),
                     pltpu.make_async_copy(kvs.at[j], kvb.at[seq], kv_recv.at[seq]),
                 )
+        whole(rs, rb_in, r_send, r_recv)
 
     def begin(here, far, near):
         @pl.when(here)
@@ -118,23 +123,31 @@
     queries = qx.shape[0]
     low = lax.broadcasted_iota(jnp.int32, (1, 2 * HEAD_DIM), 1) < HEAD_DIM
 
-    drain(qrb, qr_recv)
-    flat = qrb[...].reshape(queries, 2 * HEAD_DIM)
-    qx[...] = jnp.where(low, flat, jnp.zeros_like(flat))
+    def unpack(src, dst, keep):
+        for i in range(4):
+            both = src[i].astype(F32)
+            turned = pltpu.roll(both, HEAD_DIM, 1)
+            first, second = (both, turned) if keep else (turned, both)
+            mask = low if keep else jnp.logical_not(low)
+            dst[2 * i * BLK:(2 * i + 1) * BLK, :] = jnp.where(mask, first, 0.0).astype(BF)
+            dst[(2 * i + 1) * BLK:(2 * i + 2) * BLK, :] = jnp.where(mask, second, 0.0).astype(BF)
+
+    drain(qb, q_recv)
+    unpack(qb, qx, True)
 
     def attend(first):
         pair = kvb[pl.ds(first, 2), 0:tok, :].reshape(2 * tok, 2 * HEAD_DIM)
-        vx[...] = jnp.where(low, jnp.ones_like(pair), pair)
+        vxt[...] = jnp.where(low, jnp.ones_like(pair), pair).T
         for t in range(queries // 256):
-            rows = slice(t * 256, (t + 1) * 256)
-            scores = lax.dot_general(qx[rows, :], pair, NT, preferred_element_type=F32)
-            old = run_max[rows, :]
-            new = jnp.maximum(old, jnp.max(scores, axis=1, keepdims=True))
-            weights = jnp.exp(scores - new[:, 0:1]).astype(BF)
-            acc[rows, :] = acc[rows, :] * jnp.exp(old - new) + jnp.dot(
-                weights, vx[...], preferred_element_type=F32
+            cols = slice(t * 256, (t + 1) * 256)
+            scores = lax.dot_general(pair, qx[cols, :], NT, preferred_element_type=F32)
+            old = run_max[:, cols]
+            new = jnp.maximum(old, jnp.max(scores, axis=0, keepdims=True))
+            weights = jnp.exp(scores - new).astype(BF)
+            acc[:, cols] = acc[:, cols] * jnp.exp(old - new) + jnp.dot(
+                vxt[...], weights, preferred_element_type=F32
             )
-            run_max[rows, :] = new
+            run_max[:, cols] = new
 
     @pl.loop(0, n // 4)
     def _(i):
@@ -163,10 +176,10 @@
             for b in range(2)
         ]
 
-    total = acc[...]
-    context = (total / pltpu.roll(total, HEAD_DIM, 1)).astype(BF).astype(F32)
-    summed = (qrb[...].reshape(queries, 2 * HEAD_DIM).astype(F32) + context).astype(BF)
-    stream[...] = jnp.where(low, jnp.zeros_like(summed), summed)
+    context = (acc[HEAD_DIM:, :] / acc[0:HEAD_DIM, :]).astype(BF)
+    context = jnp.concatenate([jnp.zeros_like(context), context], axis=0)
+    drain(rb_in, r_recv)
+    unpack(rb_in, rx, False)
 
     here_first = (seq % g) * 8 + 4 * core
     here_codes = [code for i in range(4) for code in codes_of(here_first + i)]
@@ -179,7 +192,9 @@
             [jnp.where(big_rows == code - base, 1.0, 0.0).astype(BF) for code in here_codes],
             axis=1,
         )
-        part = jnp.dot(pick, stream[...], preferred_element_type=F32)
+        part = jnp.dot(pick, rx[...], preferred_element_type=F32) + lax.dot_general(
+            pick, context, NT, preferred_element_type=F32
+        )
         part = part.reshape(32, POOL, 2 * HEAD_DIM)
         upper, lower = part[:, 0:8, :], part[:, 8:16, :]
         turned = pltpu.roll(lower.reshape(256, 2 * HEAD_DIM), HEAD_DIM, 1)
@@ -324,11 +339,7 @@
     greg_ref[...] = gacc[...].astype(BF)
     mean_grad = lax.dot_general(picked.astype(BF), w_ref[...], NT, preferred_element_type=F32)
     track_grad = (mean_grad / jnp.concatenate(divisors[1:], axis=0)).astype(BF)
-    for b in range(2):
-        select = jnp.where(slot_row.astype(F32) == slots[b], 1.0, 0.0).astype(BF)
-        cgrad_ref[b * BLK:(b + 1) * BLK, :] = lax.dot_general(
-            select, track_grad[b * POOL:(b + 1) * POOL], TN, preferred_element_type=F32
-        ).astype(BF)
+    tgrad_ref[...] = track_grad
 
     first_sends(finish)
     drain(kvb.at[pl.ds(0, n // 2)], fw_send)
@@ -343,6 +354,18 @@
     drain(eb.at[0], ef_send)
 
 
+def finish_kernel(part_ref, track_ref, rc_ref, ps_ref, greg_ref, cgrad_ref):
+    greg_ref[...] = part_ref[...]
+    lane_row = lax.broadcasted_iota(jnp.int32, (1, BLK), 1)
+    slot_row = lax.broadcasted_iota(jnp.int32, (POOL, BLK), 0)
+    for b in range(2):
+        slot = jnp.where(lane_row < rc_ref[b], ps_ref[b:b + 1, :], -1)
+        select = jnp.where(slot_row == slot, 1.0, 0.0).astype(BF)
+        cgrad_ref[b * BLK:(b + 1) * BLK, :] = lax.dot_general(
+            select, track_ref[b * POOL:(b + 1) * POOL], TN, preferred_element_type=F32
+        ).astype(BF)
+
+
 def solution(mesh):
     n = mesh.shape["seq"]
     devices = 4 * n
@@ -353,25 +376,27 @@
         dma = pltpu.SemaphoreType.DMA
         vmem, smem = pl.BlockSpec(memory_space=pltpu.VMEM), pl.BlockSpec(memory_space=pltpu.SMEM)
         two = 2 * HEAD_DIM
-        return pl.pallas_call(
+        part, track_grad = pl.pallas_call(
             functools.partial(kernel, n),
             out_shape=(
                 jax.ShapeDtypeStruct((width, target_width), BF),
-                jax.ShapeDtypeStruct((tok, width), BF),
+                jax.ShapeDtypeStruct((2 * POOL, width), BF),
             ),
             in_specs=[vmem] * 6 + [smem, smem, vmem],
             out_specs=(vmem, vmem),
             scratch_shapes=[
                 pltpu.VMEM((4, tok + INFO, two), BF),
-                pltpu.VMEM((4, tok, two), BF),
+                pltpu.VMEM((4, BLK, two), BF),
+                pltpu.VMEM((4, BLK, two), BF),
                 pltpu.VMEM((n, tok + INFO, two), BF),
-                pltpu.VMEM((4, tok, two), BF),
+                pltpu.VMEM((4, BLK, two), BF),
+                pltpu.VMEM((4, BLK, two), BF),
                 pltpu.VMEM((4 * tok, two), BF),
-                pltpu.VMEM((2 * tok, two), BF),
-                pltpu.VMEM((4 * tok, two), F32),
-                pltpu.VMEM((4 * tok, two), F32),
+                pltpu.VMEM((4 * tok, two), BF),
+                pltpu.VMEM((two, 2 * tok), BF),
+                pltpu.VMEM((1, 4 * tok), F32),
+                pltpu.VMEM((two, 4 * tok), F32),
                 pltpu.VMEM((4, width, target_width), BF),
-                pltpu.VMEM((4 * tok, two), BF),
                 pltpu.VMEM((devices, 8, two), F32),
                 pltpu.VMEM((devices, 8, two), F32),
                 pltpu.VMEM((4, n // 2, POOL, width), BF),
@@ -380,6 +405,8 @@
                 pltpu.VMEM((width, target_width), F32),
                 dma((4 * (n // 8),)),
                 dma((n,)),
+                dma((4,)),
+                dma,
                 dma((4,)),
                 dma,
                 dma,
@@ -396,6 +423,15 @@
                 transcendentals=4 * tok * n * tok,
             ),
         )(queries, keys, values, residual, weight, targets, block_track, row_count, slot)
+        return pl.pallas_call(
+            finish_kernel,
+            out_shape=(
+                jax.ShapeDtypeStruct((width, target_width), BF),
+                jax.ShapeDtypeStruct((tok, width), BF),
+            ),
+            in_specs=[vmem, vmem, smem, vmem],
+            out_specs=(vmem, vmem),
+        )(part, track_grad, row_count, slot)
 
     return jax.shard_map(
         local,

time: 56 us -> 54 us (0.964)
  local copies, waits for them, and re-layouts: 2.56 us -> 0 us
  Pallas kernels: 52 us -> 52.6 us
    unnamed x4 -> x0, local copies, waits for them, and re-layouts: 2.56 us -> none
    pallas_call x0 -> x1, Pallas kernels: none -> 2.02 us  [local(): pl.pallas_call(finish_kernel, out_shape=(jax.ShapeDtypeStruct((width, tar...]
    pallas_call x1, Pallas kernels: 52 us -> 50.6 us  [local(): pl.pallas_call(functools.partial(kernel, n), out_shape=(jax.ShapeDtypeStr...]
where the time goes in v3:
time: 54 us; the launch traced here: 53.3 us
  Pallas kernels  52.6 us (97%)
  between operations  0.64 us (1%)
    pallas_call x1, Pallas kernels, local(): pl.pallas_call(functools.partial(kernel, n), out_shape=(jax.ShapeDtypeStr...  50.6 us
    pallas_call x1, Pallas kernels, local(): pl.pallas_call(finish_kernel, out_shape=(jax.ShapeDtypeStruct((width, tar...  2.02 us

profile of v3, /device:TPU:0, one launch (start us, length us, event | category | flops | bytes accessed | tf_op | source)
XLA Modules:
  0.0 53.3 jit_solution(5855796730379250049)
XLA Ops:
  0.6 50.6 %shard_map.104 = (bf16[256,1024]{1,0:T(8,128)(2,1)}, bf16[32,256]{1,0:T(8,128)(2,1)}) custom-call(bf16[256,256]{1,0:T(8,128)(2,1)} %q_ref.1, bf16[256,256]{1,0:T(8,128)(2,1)} %k_ref.1, bf16[256,256]{1,0:T(8,128)(2,1)} %v_ref.1, bf16[256,256]{1,0:T(8,128)(2,1)} %r_ref.1, bf16[256,1024]{1,0:T(8,128)(2,1)} %w_ref.1, bf16[4,16,1024]{2,1,0:T(8,128)(2,1)} %tgt_ref.1, ...), custom_call_target="tpu_custom_call" | custom-call | flops 536870912 | bytes 8388608 | tf_op jit(solution)/shard_map/pallas_call | solution.py:379
  51.3 2.0 %shard_map.105 = (bf16[256,1024]{1,0:T(8,128)(2,1)}, bf16[256,256]{1,0:T(8,128)(2,1)}) custom-call(bf16[256,1024]{1,0:T(8,128)(2,1)} %get-tuple-element.4.part_ref, bf16[32,256]{1,0:T(8,128)(2,1)} %get-tuple-element.5.track_ref, s32[2]{0:T(128)} %rc_ref.3, s32[2,128]{1,0:T(2,128)} %ps_ref.3), custom_call_target="tpu_custom_call" | custom-call | tf_op jit(solution)/shard_map/pallas_call | solution.py:426

commit v4 on v3

v4 whole, which is shorter than its diff:
```python
import functools

import jax
import jax.numpy as jnp
from jax import lax
from jax.experimental import pallas as pl
from jax.experimental.pallas import tpu as pltpu
from jax.sharding import PartitionSpec as P

HEAD_DIM = 64
BLK = 128
POOL = 16
INFO = 16
BF = jnp.bfloat16
F32 = jnp.float32
MESH = pl.DeviceIdType.MESH
NT = (((1,), (1,)), ((), ()))
TN = (((0,), (0,)), ((), ()))


def drain(ref, sem):
    pltpu.make_async_copy(ref, ref, sem).wait()


def remote(src, dst, send, recv, seq, head):
    return pltpu.make_async_remote_copy(
        src_ref=src, dst_ref=dst, send_sem=send, recv_sem=recv,
        device_id={"seq": seq, "head": head}, device_id_type=MESH,
    )


def kernel(
    n, q_ref, k_ref, v_ref, r_ref, w_ref, tgt_ref, bt_ref, rc_ref, ps_ref,
    greg_ref, tgrad_ref,
    kvs, qs, rs, kvb, qb, rb_in, qx, rx, vxt, run_max, acc, wbuf,
    row_code, row_weight, sums, parts, mb, tb, mean, picked, errors, gacc,
    kv_send, kv_recv, q_send, q_recv, r_send, r_recv, fw_send, w_send, w_recv, p_send, p_recv,
    m_send, m_recv, m2_send, m2_recv, m3_send, m3_recv,
    t_send, t_recv, t2_send, t2_recv, t3_send, t3_recv,
):
    g = n // 8
    blocks = 2 * n
    seq, head = lax.axis_index("seq"), lax.axis_index("head")
    core, yy = head % 2, head // 2
    partner, across = 2 * yy + 1 - core, (head + 2) % 4
    tok = q_ref.shape[0]
    line = n // 2
    outer, inner = seq // 2, seq % 2
    sign = 1 - 2 * (outer // (line // 2))
    block = inner * 2 + yy

    barrier = pltpu.get_barrier_semaphore()

    def greet(to_seq, to):
        pl.semaphore_signal(
            barrier, inc=1, device_id={"seq": to_seq, "head": to}, device_id_type=MESH
        )

    @pl.loop(1, 2 * n)
    def _(i):
        other = (seq * 2 + core + i) % (2 * n)
        greet(other // 2, 2 * yy + other % 2)

    for to_inner in range(2):
        greet(outer * 2 + to_inner, across)

    lane_row = lax.broadcasted_iota(jnp.int32, (1, BLK), 1)
    slots = [
        jnp.where(lane_row < rc_ref[b], ps_ref[b:b + 1, :], -1).astype(F32) for b in range(2)
    ]
    own_tracks = [bt_ref[2 * seq + b] for b in range(2)]
    row = lax.broadcasted_iota(jnp.int32, (INFO, BLK), 0)
    tracks = jnp.where(row == 2, own_tracks[0], own_tracks[1]).astype(F32)
    info = jnp.where(row == 0, slots[0], jnp.where(row == 1, slots[1], tracks)).astype(BF)
    for j in range(4):
        cols = slice(j * HEAD_DIM, (j + 1) * HEAD_DIM)
        qs[j] = jnp.concatenate([q_ref[0:BLK, cols], q_ref[BLK:, cols]], axis=1) * BF(HEAD_DIM ** -0.5)
        rs[j] = jnp.concatenate([r_ref[0:BLK, cols], r_ref[BLK:, cols]], axis=1)
        kvs[j, 0:tok, :] = jnp.concatenate([k_ref[:, cols], v_ref[:, cols]], axis=1)
        kvs[j, tok:tok + INFO, :] = info

    pl.semaphore_wait(barrier, 2 * n + 1)

    half, chunk = (seq // 4) % 2, seq // 8
    to_head = 2 * yy + half

    def first_sends(act):
        def whole(src, dst, send, recv):
            for j in range(4):
                lead = (4 * core + j) * g + chunk
                act(
                    jnp.logical_and(lead == seq, to_head == head),
                    remote(src.at[j], dst.at[seq % 4], send.at[j], recv, lead, to_head),
                    pltpu.make_async_copy(src.at[j], dst.at[seq % 4], recv),
                )

        whole(qs, qb, q_send, q_recv)
        for j in range(4):
            lead = (4 * core + j) * g
            for c in range(g):
                act(
                    jnp.logical_and(lead + c == seq, to_head == head),
                    remote(kvs.at[j], kvb.at[seq], kv_send.at[j * g + c], kv_recv.at[seq],
                           lead + c, to_head),
                    pltpu.make_async_copy(kvs.at[j], kvb.at[seq], kv_recv.at[seq]),
                )
        whole(rs, rb_in, r_send, r_recv)

    def begin(here, far, near):
        @pl.when(here)
        def _():
            near.start()

        @pl.when(jnp.logical_not(here))
        def _():
            far.start()

    def finish(here, far, near):
        @pl.when(jnp.logical_not(here))
        def _():
            far.wait_send()

    first_sends(begin)
    w_across = remote(w_ref, wbuf.at[head], w_send.at[0], w_recv.at[head], seq, across)
    w_pair = remote(w_ref, wbuf.at[head], w_send.at[1], w_recv.at[head], seq, partner)
    w_own = pltpu.make_async_copy(w_ref, wbuf.at[head], w_recv.at[head])
    w_across.start()
    w_pair.start()
    w_own.start()

    def along(i):
        return (outer + sign * i + line) % line

    def plane(d):
        return (inner + d % 2) % 2, (yy + d // 2) % 2

    def gather_along(buf, send, recv):
        own = buf.at[core, block * line + outer]

        @pl.loop(1, line)
        def _(i):
            remote(own, own, send, recv.at[outer], along(i) * 2 + inner, head).start()

    def gather_plane(buf, recv, send2, recv2):
        @pl.loop(0, line)
        def _(i):
            spot = buf.at[core, block * line + along(i)]

            @pl.when(i > 0)
            def _():
                drain(spot, recv.at[along(i)])

            for d in range(1, 4):
                to_inner, to_yy = plane(d)
                remote(
                    spot, spot, send2, recv2.at[block], outer * 2 + to_inner, 2 * to_yy + core
                ).start()

    def gather_pair(buf, recv2, send3, recv3):
        for d in range(4):
            from_inner, from_yy = plane(d)
            other = from_inner * 2 + from_yy
            spot = buf.at[core, pl.ds(other * line, line)]
            if d > 0:
                drain(spot, recv2.at[other])
            remote(spot, spot, send3, recv3.at[other], seq, partner).start()

    def gather_end(buf, recv3):
        for other in range(4):
            drain(buf.at[1 - core, pl.ds(other * line, line)], recv3.at[other])

    def gather_sent(buf, send, send2, send3):
        drain(buf.at[0, 0:line - 1], send)
        drain(buf.at[0, 0:3 * line], send2)
        drain(buf.at[0], send3)

    tb_own = tb.at[core, block * line + outer]
    tb_own[...] = tgt_ref[head]
    gather_along(tb, t_send, t_recv)

    slot_row = lax.broadcasted_iota(jnp.int32, (POOL, BLK), 0)

    def describe(b, earlier):
        track = bt_ref[b]
        row_code[b] = (track * POOL + slot_row).astype(F32)
        fresh = jnp.ones((POOL, BLK), F32)
        for other in earlier:
            fresh = jnp.where(slot_row * 0 + bt_ref[other] == track, 0.0, fresh)
        row_weight[b] = fresh

    for b in range(blocks):
        describe(b, range(b))

    run_max[...] = jnp.full_like(run_max, -1e30)
    acc[...] = jnp.zeros_like(acc)
    queries = qx.shape[0]
    low = lax.broadcasted_iota(jnp.int32, (1, 2 * HEAD_DIM), 1) < HEAD_DIM

    def unpack(src, dst, keep):
        for i in range(4):
            both = src[i].astype(F32)
            turned = pltpu.roll(both, HEAD_DIM, 1)
            first, second = (both, turned) if keep else (turned, both)
            mask = low if keep else jnp.logical_not(low)
            rest = 0.0 if keep else 1.0
            dst[2 * i * BLK:(2 * i + 1) * BLK, :] = jnp.where(mask, first, rest).astype(BF)
            dst[(2 * i + 1) * BLK:(2 * i + 2) * BLK, :] = jnp.where(mask, second, rest).astype(BF)

    drain(qb, q_recv)
    unpack(qb, qx, True)

    def attend(first):
        pair = kvb[pl.ds(first, 2), 0:tok, :].reshape(2 * tok, 2 * HEAD_DIM)
        vxt[...] = jnp.where(low, jnp.ones_like(pair), pair).T
        for t in range(queries // 256):
            cols = slice(t * 256, (t + 1) * 256)
            scores = lax.dot_general(pair, qx[cols, :], NT, preferred_element_type=F32)
            old = run_max[:, cols]
            new = jnp.maximum(old, jnp.max(scores, axis=0, keepdims=True))
            weights = jnp.exp(scores - new).astype(BF)
            acc[:, cols] = acc[:, cols] * jnp.exp(old - new) + jnp.dot(
                vxt[...], weights, preferred_element_type=F32
            )
            run_max[:, cols] = new

    @pl.loop(0, n // 4)
    def _(i):
        first = (i // 2) * 8 + 4 * core + 2 * (i % 2)
        for one in range(2):
            s = first + one
            drain(kvb.at[s], kv_recv.at[s])
            remote(kvb.at[s], kvb.at[s], fw_send, kv_recv.at[s], seq, partner).start()
        attend(first)

    drain(wbuf.at[across], w_recv.at[across])
    w_on = remote(wbuf.at[across], wbuf.at[across], w_send.at[2], w_recv.at[across], seq, partner)
    w_on.start()

    gather_plane(tb, t_recv, t2_send, t2_recv)

    @pl.loop(0, n // 4)
    def _(i):
        first = (i // 2) * 8 + 4 * (1 - core) + 2 * (i % 2)
        for one in range(2):
            drain(kvb.at[first + one], kv_recv.at[first + one])
        attend(first)

    def codes_of(s):
        lines = kvb[s, tok:tok + INFO, :].astype(F32)
        return [
            jnp.where(lines[b:b + 1] < 0, -1.0, POOL * lines[2 + b:3 + b] + lines[b:b + 1])
            for b in range(2)
        ]

    context = (acc[HEAD_DIM:, :] / acc[0:HEAD_DIM, :]).astype(BF)
    context = jnp.concatenate([jnp.zeros_like(context), context], axis=0)
    drain(rb_in, r_recv)
    unpack(rb_in, rx, False)

    here_first = (seq % g) * 8 + 4 * core
    here_codes = [code for i in range(4) for code in codes_of(here_first + i)]

    @pl.loop(0, n // 8)
    def _(i):
        code_rows = row_code[pl.ds(16 * i, 16)].reshape(256, BLK)
        pick = jnp.concatenate(
            [jnp.where(code_rows == code, 1.0, 0.0).astype(BF) for code in here_codes], axis=1
        )
        both = jnp.dot(pick, rx[...], preferred_element_type=F32) + lax.dot_general(
            pick, context, NT, preferred_element_type=F32
        )
        sums[pl.ds(2 * i, 2)] = both.reshape(2, BLK, 2 * HEAD_DIM)

    members = 2 * g
    lead = seq // g * g
    rank = seq % g * 2 + core

    for i in range(1, members):
        to = (rank + i) % members
        remote(
            sums.at[to], parts.at[members - 1 - i], p_send, p_recv, lead + to // 2, 2 * yy + to % 2
        ).start()

    gather_pair(tb, t2_recv, t3_send, t3_recv)
    drain(parts.at[0:members - 1], p_recv)
    whole_sum = sums[rank]
    for i in range(members - 1):
        whole_sum = whole_sum + parts[i]
    turned = pltpu.roll(whole_sum, HEAD_DIM, 1)
    wide = jnp.where(low, whole_sum, turned)
    own_mean = jnp.where(low, turned, whole_sum) / jnp.maximum(wide, 1.0)
    half_rows = BLK // 2
    mb_own = mb.at[core, block * line + outer]
    mb_own[...] = jnp.where(
        low, own_mean[half_rows:], own_mean[0:half_rows]
    ).astype(BF)
    gather_along(mb, m_send, m_recv)

    gather_end(tb, t3_recv)

    @pl.loop(0, n // 8)
    def _(i):
        code_rows = row_code[pl.ds(16 * i, 16)].reshape(256, BLK)[:, 0:1]
        spot = lax.broadcasted_iota(jnp.int32, (256, 32 * n), 1)
        place = spot // POOL
        found = None
        for side in (core, 1 - core):
            track = 4 * (2 * (place % line) + place // (2 * line)) + 2 * (place // line % 2) + side
            code = (track * POOL + spot % POOL).astype(F32)
            pick = jnp.where(code == code_rows, 1.0, 0.0).astype(BF)
            term = jnp.dot(pick, tb[side].reshape(32 * n, -1), preferred_element_type=F32)
            found = term if found is None else found + term
        picked[i] = found.astype(BF)

    wanted = [(t * POOL + slot_row).astype(F32) for t in own_tracks]

    def add_counts(s, totals):
        codes = codes_of(s)
        return tuple(
            total + jnp.where(want == codes[0], 1.0, 0.0) + jnp.where(want == codes[1], 1.0, 0.0)
            for total, want in zip(totals, wanted)
        )

    zero = jnp.zeros((POOL, BLK), F32)
    counts = lax.fori_loop(0, n, add_counts, (zero, zero))
    divisors = [jnp.maximum(jnp.sum(c, axis=1, keepdims=True), 1.0) for c in counts]
    for k in range(2):
        drain(wbuf.at[2 * yy + k], w_recv.at[2 * yy + k])
    drain(wbuf.at[2 * (1 - yy) + 1 - core], w_recv.at[2 * (1 - yy) + 1 - core])

    gather_plane(mb, m_recv, m2_send, m2_recv)
    gather_pair(mb, m2_recv, m3_send, m3_recv)
    gather_end(mb, m3_recv)

    for part in range(members):
        side, share = (core if part % 2 == 0 else 1 - core), part // 2
        for pair in range(8):
            two = []
            for hd in (2 * pair, 2 * pair + 1):
                y, s = hd // 8, hd % 8 * g + share
                two.append(mb[side, (s % 2 * 2 + y) * line + s // 2].astype(F32))
            a, b = two
            at = slice(pair % 2 * BLK, pair % 2 * BLK + BLK)
            mean[pair // 2, share, side, 0:half_rows, at] = jnp.where(
                low, pltpu.roll(a, HEAD_DIM, 1), b
            ).astype(BF)
            mean[pair // 2, share, side, half_rows:BLK, at] = jnp.where(
                low, a, pltpu.roll(b, HEAD_DIM, 1)
            ).astype(BF)

    @pl.loop(0, n // 8)
    def _(i):
        prediction = jnp.dot(mean[0, i].reshape(256, -1), wbuf[0], preferred_element_type=F32)
        for k in range(1, 4):
            prediction += jnp.dot(mean[k, i].reshape(256, -1), wbuf[k], preferred_element_type=F32)
        error = (prediction - picked[i].astype(F32)).astype(BF)
        errors[pl.ds(8 * i, 8)] = error.reshape(8, 2 * POOL, -1)
        weight = row_weight[pl.ds(16 * i, 16)].reshape(256, BLK)[:, 0:1]
        once = (mean[head, i].reshape(256, -1).astype(F32) * weight).astype(BF)
        term = lax.dot_general(once, error, TN, preferred_element_type=F32)
        gacc[...] = term + jnp.where(i > 0, gacc[...], 0.0)

    greg_ref[...] = gacc[...].astype(BF)
    mean_grad = lax.dot_general(errors[seq], w_ref[...], NT, preferred_element_type=F32)
    tgrad_ref[...] = (mean_grad / jnp.concatenate(divisors, axis=0)).astype(BF)

    first_sends(finish)
    drain(kvb.at[pl.ds(0, n // 2)], fw_send)
    w_across.wait_send()
    w_pair.wait_send()
    w_on.wait_send()
    drain(sums.at[pl.ds(0, members - 1)], p_send)
    gather_sent(mb, m_send, m2_send, m3_send)
    gather_sent(tb, t_send, t2_send, t3_send)


def finish_kernel(part_ref, track_ref, rc_ref, ps_ref, greg_ref, cgrad_ref):
    greg_ref[...] = part_ref[...]
    lane_row = lax.broadcasted_iota(jnp.int32, (1, BLK), 1)
    slot_row = lax.broadcasted_iota(jnp.int32, (POOL, BLK), 0)
    for b in range(2):
        slot = jnp.where(lane_row < rc_ref[b], ps_ref[b:b + 1, :], -1)
        select = jnp.where(slot_row == slot, 1.0, 0.0).astype(BF)
        cgrad_ref[b * BLK:(b + 1) * BLK, :] = lax.dot_general(
            select, track_ref[b * POOL:(b + 1) * POOL], TN, preferred_element_type=F32
        ).astype(BF)


def solution(mesh):
    n = mesh.shape["seq"]
    members = n // 4

    def local(queries, keys, values, residual, weight, targets, block_track, row_count, slot):
        tok, width = queries.shape
        target_width = weight.shape[1]
        dma = pltpu.SemaphoreType.DMA
        vmem, smem = pl.BlockSpec(memory_space=pltpu.VMEM), pl.BlockSpec(memory_space=pltpu.SMEM)
        two = 2 * HEAD_DIM
        part, track_grad = pl.pallas_call(
            functools.partial(kernel, n),
            out_shape=(
                jax.ShapeDtypeStruct((width, target_width), BF),
                jax.ShapeDtypeStruct((2 * POOL, width), BF),
            ),
            in_specs=[vmem] * 6 + [smem, smem, vmem],
            out_specs=(vmem, vmem),
            scratch_shapes=[
                pltpu.VMEM((4, tok + INFO, two), BF),
                pltpu.VMEM((4, BLK, two), BF),
                pltpu.VMEM((4, BLK, two), BF),
                pltpu.VMEM((n, tok + INFO, two), BF),
                pltpu.VMEM((4, BLK, two), BF),
                pltpu.VMEM((4, BLK, two), BF),
                pltpu.VMEM((4 * tok, two), BF),
                pltpu.VMEM((4 * tok, two), BF),
                pltpu.VMEM((two, 2 * tok), BF),
                pltpu.VMEM((1, 4 * tok), F32),
                pltpu.VMEM((two, 4 * tok), F32),
                pltpu.VMEM((4, width, target_width), BF),
                pltpu.VMEM((2 * n, POOL, BLK), F32),
                pltpu.VMEM((2 * n, POOL, BLK), F32),
                pltpu.VMEM((members, BLK, two), F32),
                pltpu.VMEM((members - 1, BLK, two), F32),
                pltpu.VMEM((2, 2 * n, BLK // 2, two), BF),
                pltpu.VMEM((2, 2 * n, POOL, target_width), BF),
                pltpu.VMEM((4, n // 8, 2, BLK, width), BF),
                pltpu.VMEM((n // 8, 256, target_width), BF),
                pltpu.VMEM((n, 2 * POOL, target_width), BF),
                pltpu.VMEM((width, target_width), F32),
                dma((4 * (n // 8),)),
                dma((n,)),
                dma((4,)),
                dma,
                dma((4,)),
                dma,
                dma,
                dma((3,)),
                dma((4,)),
                dma, dma,
                dma, dma((n // 2,)), dma, dma((4,)), dma, dma((4,)),
                dma, dma((n // 2,)), dma, dma((4,)), dma, dma((4,)),
            ],
            compiler_params=pltpu.CompilerParams(
                collective_id=0, has_side_effects=True, vmem_limit_bytes=56 * 1024 * 1024
            ),
            cost_estimate=pl.CostEstimate(
                flops=4 * 4 * tok * n * tok * HEAD_DIM, bytes_accessed=8 * 1024 * 1024,
                transcendentals=4 * tok * n * tok,
            ),
        )(queries, keys, values, residual, weight, targets, block_track, row_count, slot)
        return pl.pallas_call(
            finish_kernel,
            out_shape=(
                jax.ShapeDtypeStruct((width, target_width), BF),
                jax.ShapeDtypeStruct((tok, width), BF),
            ),
            in_specs=[vmem, vmem, smem, vmem],
            out_specs=(vmem, vmem),
        )(part, track_grad, row_count, slot)

    return jax.shard_map(
        local,
        mesh=mesh,
        in_specs=(
            P("seq", "head"),
            P("seq", "head"),
            P("seq", "head"),
            P("seq", "head"),
            P("head", None),
            P("seq", None, None),
            P(),
            P("seq"),
            P("seq", None),
        ),
        out_specs=(P("head", None), P("seq", "head")),
        check_vma=False,
    )
```

time: 54 us -> 44.1 us (0.82)
  Pallas kernels: 52.6 us -> 42.7 us
    pallas_call x1, Pallas kernels: 50.6 us -> 40.7 us  [local(): pl.pallas_call(functools.partial(kernel, n), out_shape=(jax.ShapeDtypeStr...]
where the time goes in v4:
time: 44.1 us; the launch traced here: 43.3 us
  Pallas kernels  42.7 us (97%)
  between operations  0.64 us (1%)
    pallas_call x1, Pallas kernels, local(): pl.pallas_call(functools.partial(kernel, n), out_shape=(jax.ShapeDtypeStr...  40.7 us
    pallas_call x1, Pallas kernels, local(): pl.pallas_call(finish_kernel, out_shape=(jax.ShapeDtypeStruct((width, tar...  2.02 us

profile of v4, /device:TPU:0, one launch (start us, length us, event | category | flops | bytes accessed | tf_op | source)
XLA Modules:
  0.0 43.3 jit_solution(16817146205955889513)
XLA Ops:
  0.6 40.7 %shard_map.104 = (bf16[256,1024]{1,0:T(8,128)(2,1)}, bf16[32,256]{1,0:T(8,128)(2,1)}) custom-call(bf16[256,256]{1,0:T(8,128)(2,1)} %q_ref.1, bf16[256,256]{1,0:T(8,128)(2,1)} %k_ref.1, bf16[256,256]{1,0:T(8,128)(2,1)} %v_ref.1, bf16[256,256]{1,0:T(8,128)(2,1)} %r_ref.1, bf16[256,1024]{1,0:T(8,128)(2,1)} %w_ref.1, bf16[4,16,1024]{2,1,0:T(8,128)(2,1)} %tgt_ref.1, ...), custom_call_target="tpu_custom_call" | custom-call | flops 536870912 | bytes 8388608 | tf_op jit(solution)/shard_map/pallas_call | solution.py:399
  41.3 2.0 %shard_map.105 = (bf16[256,1024]{1,0:T(8,128)(2,1)}, bf16[256,256]{1,0:T(8,128)(2,1)}) custom-call(bf16[256,1024]{1,0:T(8,128)(2,1)} %get-tuple-element.4.part_ref, bf16[32,256]{1,0:T(8,128)(2,1)} %get-tuple-element.5.track_ref, s32[2]{0:T(128)} %rc_ref.3, s32[2,128]{1,0:T(2,128)} %ps_ref.3), custom_call_target="tpu_custom_call" | custom-call | tf_op jit(solution)/shard_map/pallas_call | solution.py:451

commit v5 on v4

--- a/solution.py
+++ b/solution.py
@@ -296,6 +296,24 @@
     ).astype(BF)
     gather_along(mb, m_send, m_recv)
 
+    wanted = [(t * POOL + slot_row).astype(F32) for t in own_tracks]
+
+    def add_counts(s, totals):
+        codes = codes_of(s)
+        return tuple(
+            total + jnp.where(want == codes[0], 1.0, 0.0) + jnp.where(want == codes[1], 1.0, 0.0)
+            for total, want in zip(totals, wanted)
+        )
+
+    zero = jnp.zeros((POOL, BLK), F32)
+    counts = lax.fori_loop(0, n, add_counts, (zero, zero))
+    divisors = [jnp.maximum(jnp.sum(c, axis=1, keepdims=True), 1.0) for c in counts]
+    for k in range(2):
+        drain(wbuf.at[2 * yy + k], w_recv.at[2 * yy + k])
+    drain(wbuf.at[2 * (1 - yy) + 1 - core], w_recv.at[2 * (1 - yy) + 1 - core])
+
+    gather_plane(mb, m_recv, m2_send, m2_recv)
+
     gather_end(tb, t3_recv)
 
     @pl.loop(0, n // 8)
@@ -312,23 +330,6 @@
             found = term if found is None else found + term
         picked[i] = found.astype(BF)
 
-    wanted = [(t * POOL + slot_row).astype(F32) for t in own_tracks]
-
-    def add_counts(s, totals):
-        codes = codes_of(s)
-        return tuple(
-            total + jnp.where(want == codes[0], 1.0, 0.0) + jnp.where(want == codes[1], 1.0, 0.0)
-            for total, want in zip(totals, wanted)
-        )
-
-    zero = jnp.zeros((POOL, BLK), F32)
-    counts = lax.fori_loop(0, n, add_counts, (zero, zero))
-    divisors = [jnp.maximum(jnp.sum(c, axis=1, keepdims=True), 1.0) for c in counts]
-    for k in range(2):
-        drain(wbuf.at[2 * yy + k], w_recv.at[2 * yy + k])
-    drain(wbuf.at[2 * (1 - yy) + 1 - core], w_recv.at[2 * (1 - yy) + 1 - core])
-
-    gather_plane(mb, m_recv, m2_send, m2_recv)
     gather_pair(mb, m2_recv, m3_send, m3_recv)
     gather_end(mb, m3_recv)
 

time: 44.1 us -> 44.1 us (level)
  no operation moved by 1% of the time
where the time goes in v5:
time: 44.1 us; the launch traced here: 43.3 us
  Pallas kernels  42.7 us (97%)
  between operations  0.64 us (1%)
    pallas_call x1, Pallas kernels, local(): pl.pallas_call(functools.partial(kernel, n), out_shape=(jax.ShapeDtypeStr...  40.7 us
    pallas_call x1, Pallas kernels, local(): pl.pallas_call(finish_kernel, out_shape=(jax.ShapeDtypeStruct((width, tar...  2.02 us

profile of v5, /device:TPU:0, one launch (start us, length us, event | category | flops | bytes accessed | tf_op | source)
XLA Modules:
  0.0 43.3 jit_solution(7780268980110446928)
XLA Ops:
  0.6 40.7 %shard_map.104 = (bf16[256,1024]{1,0:T(8,128)(2,1)}, bf16[32,256]{1,0:T(8,128)(2,1)}) custom-call(bf16[256,256]{1,0:T(8,128)(2,1)} %q_ref.1, bf16[256,256]{1,0:T(8,128)(2,1)} %k_ref.1, bf16[256,256]{1,0:T(8,128)(2,1)} %v_ref.1, bf16[256,256]{1,0:T(8,128)(2,1)} %r_ref.1, bf16[256,1024]{1,0:T(8,128)(2,1)} %w_ref.1, bf16[4,16,1024]{2,1,0:T(8,128)(2,1)} %tgt_ref.1, ...), custom_call_target="tpu_custom_call" | custom-call | flops 536870912 | bytes 8388608 | tf_op jit(solution)/shard_map/pallas_call | solution.py:400
  41.3 2.0 %shard_map.105 = (bf16[256,1024]{1,0:T(8,128)(2,1)}, bf16[256,256]{1,0:T(8,128)(2,1)}) custom-call(bf16[256,1024]{1,0:T(8,128)(2,1)} %get-tuple-element.4.part_ref, bf16[32,256]{1,0:T(8,128)(2,1)} %get-tuple-element.5.track_ref, s32[2]{0:T(128)} %rc_ref.3, s32[2,128]{1,0:T(2,128)} %ps_ref.3), custom_call_target="tpu_custom_call" | custom-call | tf_op jit(solution)/shard_map/pallas_call | solution.py:452
